TPU v7x, 512 devices: a whole 4x8x8 slice. The times are simulated.
512 devices in a mesh: gy: 4 (over z_hi, core), gx: 4 (over z_lo), dp: 32 (over x, y).
Axes of the slice: x: 4, y: 8, z: 8 (z_hi: 2, z_lo: 4; z = z_hi * 4 + z_lo), core: 2. Of those that a mesh axis runs over, the one named last changes fastest.
Arguments:
- tokens: bfloat16 [32, 4, 4, 128, 512], P('dp', 'gy', 'gx'), may hold values from -6 to 6
- tile_ids: int32 [32, 4, 4, 2], P('dp'), may hold values from -1 to 15, as said below
- w_qkv: bfloat16 [512, 768], P('dp'), may hold values from -0.25 to 0.25
- w_out: bfloat16 [256, 512], P('dp'), may hold values from -0.75 to 0.75
- norm_gain: float32 [512], replicated, may hold values from 0.1 to 1.9
- rel_bias: float32 [8, 49], replicated, may hold values from -2 to 304
- update_grad: bfloat16 [32, 4, 4, 128, 512], P('dp', 'gy', 'gx'), may hold values from -6 to 6
Outputs:
- update: bfloat16 [32, 4, 4, 128, 512], P('dp', 'gy', 'gx')
- grad_tokens: bfloat16 [32, 4, 4, 128, 512], P('dp', 'gy', 'gx')
- grad_qkv: float32 [512, 768], P('dp')
- grad_out: float32 [256, 512], P('dp')
- grad_gain: float32 [512], replicated
- grad_bias: float32 [8, 49], replicated
Inputs may be any that keep to these rules, and one draw needn't show every extreme that they name: `tile_ids`: for each crop and device the slots first hold distinct tiles of that device's region, numbered row by row with 4 to a row, then -1; each device lists exactly 2 tiles, so no slot holds -1.
All inputs are finite; a program needn't handle non-finite values.
Results may differ from a plain program's by a relative error of at most 0.027.
Values may be sent and summed in bfloat16 or wider, within the bound.
No kernel may reach another device: no remote copies, remote signals or barrier semaphores. Data moves between devices by JAX's collectives and lax.ppermute only.
A program may use at most 64 MiB of HBM per device.

v0:
```python
import jax
import jax.numpy as jnp
from jax import lax
from jax.sharding import PartitionSpec as P

D = 512
HEADS = 8
HD = 32
INNER = 256
TILE = 8
WIN = 7
HALO = 3
REG = 4
SIDE = 32
CAP = 2
ROWS = 128


def padded_2(array, sides, width):
    for axis, dim in sides:
        size, length = (lax.axis_size(axis), array.shape[dim])
        up = [(i, (i + 1) % size) for i in range(size - 1)]
        down = [(j, i) for i, j in up]
        last = lax.slice_in_dim(array, length - width, length, axis=dim)
        first = lax.slice_in_dim(array, 0, width, axis=dim)
        before = lax.ppermute(last, axis, up)
        after = lax.ppermute(first, axis, down)
        array = jnp.concatenate([before, array, after], axis=dim)
    return array


def window_tables():
    win_side = TILE + 2 * HALO
    query_cells = jnp.arange(TILE * TILE, dtype=jnp.int32)
    window_cells = jnp.arange(win_side * win_side, dtype=jnp.int32)
    row_step = (window_cells // win_side)[None, :] - HALO - (query_cells // TILE)[:, None]
    col_step = (window_cells % win_side)[None, :] - HALO - (query_cells % TILE)[:, None]
    inside = (jnp.abs(row_step) <= HALO) & (jnp.abs(col_step) <= HALO)
    offset = (row_step + HALO) * WIN + col_step + HALO
    onehot = (
        (offset[None, :, :] == jnp.arange(WIN * WIN, dtype=jnp.int32)[:, None, None])
        & inside[None, :, :]
    ).astype(jnp.float32)
    return (inside, onehot)


def softmax_scores(queries, key_rows, bias_table, allowed):
    scores = (
        jnp.einsum("nqhd,nkhd->nhqk", queries, key_rows, preferred_element_type=jnp.float32)
        * HD ** (-0.5)
        + bias_table[None]
    )
    scores = jnp.where(allowed, scores, -jnp.inf)
    row_max = jnp.max(scores, axis=-1, keepdims=True)
    exponent = jnp.exp(scores - row_max)
    return exponent / jnp.sum(exponent, axis=-1, keepdims=True)


def shards(tokens, tile_ids, w_qkv, w_out, norm_gain, rel_bias, update_grad):
    grid_high = lax.axis_size("gy")
    grid_wide = lax.axis_size("gx")
    my_row = lax.axis_index("gy")
    my_col = lax.axis_index("gx")
    win_side = TILE + 2 * HALO
    win_cells = win_side * win_side
    padded = SIDE + 2 * HALO
    block_slots = CAP
    block_count = CAP // block_slots
    inside, onehot = window_tables()
    bias_table = jnp.einsum("ho,oqk->hqk", rel_bias, onehot, precision=lax.Precision.HIGHEST)
    w_qkv_all, w_out_all = (
        lax.all_gather(w_qkv, "dp", axis=0, tiled=True),
        lax.all_gather(w_out, "dp", axis=0, tiled=True),
    )
    features = tokens.reshape(ROWS, D).astype(jnp.float32)
    inv_rms = lax.rsqrt(jnp.mean(features * features, axis=-1, keepdims=True) + 1e-06)
    normed = (features * inv_rms * norm_gain).astype(jnp.bfloat16)
    qkv_rows = jnp.dot(normed, w_qkv_all, preferred_element_type=jnp.float32).astype(jnp.bfloat16)
    crop_tiles = tile_ids.reshape(grid_high, grid_wide, CAP)
    slot_tiles = crop_tiles[my_row, my_col]
    is_active = slot_tiles >= 0
    tile_index = jnp.where(is_active, slot_tiles, 0)
    spare_local = REG * REG
    kv_tiles = qkv_rows[:, INNER:].reshape(CAP, TILE * TILE, 2 * INNER)
    tile_grid = (
        jnp.zeros((spare_local + 1, TILE * TILE, 2 * INNER), jnp.bfloat16)
        .at[jnp.where(is_active, slot_tiles, spare_local)]
        .set(kv_tiles)[:spare_local]
    )
    kv_region = (
        tile_grid.reshape(REG, REG, TILE, TILE, 2 * INNER)
        .transpose(0, 2, 1, 3, 4)
        .reshape(SIDE, SIDE, 2 * INNER)
    )
    kv_padded = padded_2(kv_region, (("gy", 0), ("gx", 1)), HALO)
    spare_tile = grid_high * REG * grid_wide * REG
    row_of_dev = jnp.arange(grid_high, dtype=jnp.int32)[:, None, None]
    col_of_dev = jnp.arange(grid_wide, dtype=jnp.int32)[None, :, None]
    flat_tiles = jnp.where(
        crop_tiles >= 0,
        (row_of_dev * REG + crop_tiles // REG) * (grid_wide * REG)
        + col_of_dev * REG
        + crop_tiles % REG,
        spare_tile,
    )
    crop_active = (
        jnp.zeros((spare_tile + 1,), jnp.float32)
        .at[flat_tiles.reshape(-1)]
        .set(1.0)[:spare_tile]
        .reshape(grid_high * REG, grid_wide * REG)
    )
    crop_active = jnp.pad(crop_active, 1)
    nearby = lax.dynamic_slice(crop_active, (my_row * REG, my_col * REG), (REG + 2, REG + 2))
    near_cells = jnp.repeat(jnp.repeat(nearby, TILE, axis=0), TILE, axis=1)
    key_active = (
        near_cells[TILE - HALO : TILE - HALO + padded, TILE - HALO : TILE - HALO + padded] > 0.5
    )
    start_rows = tile_index // REG * TILE
    start_cols = tile_index % REG * TILE
    zero_index = jnp.zeros((), jnp.int32)
    kv_windows = jax.vmap(
        lambda first_row, first_col: lax.dynamic_slice(
            kv_padded, (first_row, first_col, zero_index), (win_side, win_side, 2 * INNER)
        )
    )(start_rows, start_cols).reshape(CAP, win_cells, 2 * INNER)
    key_windows = jax.vmap(
        lambda first_row, first_col: lax.dynamic_slice(
            key_active, (first_row, first_col), (win_side, win_side)
        )
    )(start_rows, start_cols).reshape(CAP, win_cells)
    queries = qkv_rows[:, :INNER].reshape(block_count, block_slots, TILE * TILE, HEADS, HD)
    key_rows = kv_windows[:, :, :INNER].reshape(block_count, block_slots, win_cells, HEADS, HD)
    values = kv_windows[:, :, INNER:].reshape(block_count, block_slots, win_cells, HEADS, HD)
    allowed = (
        inside[None, None] & (key_windows[:, None, None, :] | ~is_active[:, None, None, None])
    ).reshape(block_count, block_slots, 1, TILE * TILE, win_cells)
    live = is_active.astype(jnp.float32).reshape(block_count, block_slots)

    def block_forward(block_items):
        query_block, key_block, value_block, allow_block, live_block = block_items
        attn_probs = softmax_scores(query_block, key_block, bias_table, allow_block)
        probs_bf = attn_probs.astype(jnp.bfloat16)
        attended = jnp.einsum(
            "nhqk,nkhd->nqhd", probs_bf, value_block, preferred_element_type=jnp.float32
        )
        return (attended * live_block[:, None, None, None]).astype(jnp.bfloat16)

    attended = lax.map(block_forward, (queries, key_rows, values, allowed, live)).reshape(
        ROWS, INNER
    )
    update = jnp.dot(attended, w_out_all, preferred_element_type=jnp.float32).astype(jnp.bfloat16)
    row_active = jnp.repeat(is_active, TILE * TILE)
    grad_rows = jnp.where(
        row_active[:, None], update_grad.reshape(ROWS, D), jnp.zeros((), jnp.bfloat16)
    )
    grad_attended = lax.dot_general(
        grad_rows, w_out_all, (((1,), (1,)), ((), ())), preferred_element_type=jnp.float32
    ).astype(jnp.bfloat16)
    grad_out_local = lax.dot_general(
        attended, grad_rows, (((0,), (0,)), ((), ())), preferred_element_type=jnp.float32
    )
    grad_heads = grad_attended.reshape(block_count, block_slots, TILE * TILE, HEADS, HD)

    def block_backward(block_items):
        query_block, key_block, value_block, allow_block, grad_block = block_items
        attn_probs = softmax_scores(query_block, key_block, bias_table, allow_block)
        probs_bf = attn_probs.astype(jnp.bfloat16)
        d_probs = jnp.einsum(
            "nqhd,nkhd->nhqk", grad_block, value_block, preferred_element_type=jnp.float32
        )
        row_delta = jnp.sum(attn_probs * d_probs, axis=-1, keepdims=True)
        d_scores = (attn_probs * (d_probs - row_delta)).astype(jnp.bfloat16)
        d_queries = jnp.einsum(
            "nhqk,nkhd->nqhd", d_scores, key_block, preferred_element_type=jnp.float32
        ) * HD ** (-0.5)
        d_keys = jnp.einsum(
            "nhqk,nqhd->nkhd", d_scores, query_block, preferred_element_type=jnp.float32
        ) * HD ** (-0.5)
        d_values = jnp.einsum(
            "nhqk,nqhd->nkhd", probs_bf, grad_block, preferred_element_type=jnp.float32
        )
        slot_part = d_keys.shape[0]
        d_kv = jnp.concatenate(
            [
                d_keys.reshape(slot_part, win_cells, INNER),
                d_values.reshape(slot_part, win_cells, INNER),
            ],
            axis=-1,
        )
        return (
            d_queries.reshape(slot_part, TILE * TILE, INNER),
            d_kv,
            jnp.sum(d_scores, axis=0, dtype=jnp.float32),
        )

    d_queries, d_kv_windows, bias_parts = lax.map(
        block_backward, (queries, key_rows, values, allowed, grad_heads)
    )
    grad_bias_sum = jnp.sum(bias_parts, axis=0)
    cell_index = jnp.arange(win_cells, dtype=jnp.int32)
    targets = (
        (start_rows[:, None] + cell_index[None, :] // win_side) * padded
        + start_cols[:, None]
        + cell_index[None, :] % win_side
    )
    grad_padded = (
        jnp.zeros((padded * padded, 2 * INNER), jnp.float32)
        .at[targets.reshape(-1)]
        .add(d_kv_windows.reshape(CAP * win_cells, 2 * INNER))
        .reshape(padded, padded, 2 * INNER)
    )
    returned = padded_2(grad_padded.astype(jnp.bfloat16), (("gy", 0), ("gx", 1)), HALO).astype(
        grad_padded.dtype
    )
    start_in = 2 * HALO
    start_far = padded + HALO
    own_grad = grad_padded[HALO : HALO + SIDE, HALO : HALO + SIDE]
    own_grad = own_grad.at[:HALO, :].add(returned[:HALO, start_in : start_in + SIDE])
    own_grad = own_grad.at[SIDE - HALO :, :].add(returned[start_far:, start_in : start_in + SIDE])
    own_grad = own_grad.at[:, :HALO].add(returned[start_in : start_in + SIDE, :HALO])
    own_grad = own_grad.at[:, SIDE - HALO :].add(returned[start_in : start_in + SIDE, start_far:])
    own_grad = own_grad.at[:HALO, :HALO].add(returned[:HALO, :HALO])
    own_grad = own_grad.at[:HALO, SIDE - HALO :].add(returned[:HALO, start_far:])
    own_grad = own_grad.at[SIDE - HALO :, :HALO].add(returned[start_far:, :HALO])
    own_grad = own_grad.at[SIDE - HALO :, SIDE - HALO :].add(returned[start_far:, start_far:])
    grad_tiles = (
        own_grad.reshape(REG, TILE, REG, TILE, 2 * INNER)
        .transpose(0, 2, 1, 3, 4)
        .reshape(REG * REG, TILE * TILE, 2 * INNER)
    )
    grad_slots = jnp.where(is_active[:, None, None], grad_tiles[tile_index], 0.0)
    grad_qkv_rows = jnp.concatenate(
        [d_queries.reshape(ROWS, INNER), grad_slots.reshape(ROWS, 2 * INNER)], axis=-1
    ).astype(jnp.bfloat16)
    grad_qkv_local = lax.dot_general(
        normed, grad_qkv_rows, (((0,), (0,)), ((), ())), preferred_element_type=jnp.float32
    )
    grad_normed = lax.dot_general(
        grad_qkv_rows, w_qkv_all, (((1,), (1,)), ((), ())), preferred_element_type=jnp.float32
    )
    scaled_grad = grad_normed * norm_gain
    gain_local = jnp.sum(grad_normed * features * inv_rms, axis=0)
    grad_tokens = (
        inv_rms * scaled_grad
        - features * inv_rms**3 * jnp.mean(scaled_grad * features, axis=-1, keepdims=True)
    ).astype(jnp.bfloat16)
    bias_local = jnp.einsum("hqk,oqk->ho", grad_bias_sum, onehot, precision=lax.Precision.HIGHEST)
    grad_gain, grad_bias = lax.psum((gain_local, bias_local), ("gy", "gx", "dp"))
    qkv_whole, out_whole = (
        lax.psum(grad_qkv_local.astype(jnp.bfloat16), ("gy", "gx")).astype(jnp.float32),
        lax.psum(grad_out_local.astype(jnp.bfloat16), ("gy", "gx")).astype(jnp.float32),
    )
    grad_qkv, grad_out = (
        lax.psum_scatter(
            qkv_whole.astype(jnp.bfloat16), "dp", scatter_dimension=0, tiled=True
        ).astype(jnp.float32),
        lax.psum_scatter(
            out_whole.astype(jnp.bfloat16), "dp", scatter_dimension=0, tiled=True
        ).astype(jnp.float32),
    )
    return (
        update.reshape(tokens.shape),
        grad_tokens.reshape(tokens.shape),
        grad_qkv,
        grad_out,
        grad_gain,
        grad_bias,
    )


def solution(mesh):
    return jax.shard_map(
        shards,
        mesh=mesh,
        in_specs=(
            P("dp", "gy", "gx", None, None),
            P("dp", None, None, None),
            P("dp", None),
            P("dp", None),
            P(),
            P(),
            P("dp", "gy", "gx", None, None),
        ),
        out_specs=(
            P("dp", "gy", "gx", None, None),
            P("dp", "gy", "gx", None, None),
            P("dp", None),
            P("dp", None),
            P(),
            P(),
        ),
        check_vma=False,
    )
```

profile of v0, /device:TPU:1, one launch (start us, length us, event | category | flops | bytes accessed | tf_op | source)
XLA Modules:
  0.0 688.9 jit_solution(10179969984633198570)
XLA Ops:
  7.2 1.0 fusion.29
  8.8 0.9 dynamic-slice_reduce_fusion
  9.7 40.1 %all_gather.6 = bf16[512,768]{1,0:T(8,128)(2,1)S(1)} all-gather(bf16[16,768]{1,0:T(8,128)(2,1)} %param.25), channel_id=1, replica_groups=mesh['gy'=4,'gx'=4,'dp'=32] {'dp'}, dimensions={0}, use_global_device_ids=true | all-gather | bytes 811008 | tf_op jit(solution)/shard_map/all_gather | solution.py:72
  49.8 1.3 convolution_convert_fusion.2
  52.2 22.8 %collective-permute-start = (bf16[3,32,512]{2,1,0:T(8,128)(2,1)S(1)}, bf16[3,32,512]{2,1,0:T(8,128)(2,1)S(1)}, u32[]{:S(2)}, u32[]{:S(2)}) collective-permute-start(bf16[3,32,512]{2,1,0:T(8,128)(2,1)S(1)} %get-tuple-element.240), channel_id=1, source_target_pairs={{0,128},{128,256},{256,384},{1,129},{129,257},{257,385},{2,130},{1... | collective-permute-start | bytes 294920 | tf_op jit(solution)/shard_map/ppermute | solution.py:26
  75.0 1.9 collective-permute-start.1
  79.4 0.7 scatter_custom_fusion.1
  80.6 4.2 while.21
  81.2 1.4 dynamic-slice.90
  83.3 1.4 dynamic-slice.90
  84.9 35.8 %all_gather.7 = bf16[256,512]{1,0:T(8,128)(2,1)S(1)} all-gather(bf16[8,512]{1,0:T(8,128)(2,1)S(1)} %copy-done.20), channel_id=1, replica_groups=mesh['gy'=4,'gx'=4,'dp'=32] {'dp'}, dimensions={0}, use_global_device_ids=true | all-gather | bytes 270336 | tf_op jit(solution)/shard_map/all_gather | solution.py:73
  120.8 0.7 broadcast_and_fusion
  121.4 1.4 fusion.16
  123.3 2.8 collective-permute-start.2
  126.1 1.5 collective-permute-start.3
  127.8 0.8 squeeze.42
  129.0 0.7 and_reduce_fusion
  129.7 0.7 copy-done.12
  130.4 1.8 collective-permute-done.3
  132.1 1.9 pad_maximum_fusion
  134.0 5.5 while.20
  134.7 2.1 bitcast_dynamic-update-slice_fusion.4
  137.4 2.1 bitcast_dynamic-update-slice_fusion.4
  139.5 1.5 copy.67
  142.3 0.8 convolution_bitcast_fusion
  144.1 0.8 fusion.23
  145.1 0.7 reshape.1052
  146.3 1.2 convert_reduce_fusion
  148.6 1.2 copy.85
  149.9 4.2 scatter_custom_fusion.2
  154.0 2.0 reshape.1056
  156.0 2.1 convert_element_type.82
  158.1 21.3 %collective-permute-start.4 = (bf16[3,38,512]{2,1,0:T(8,128)(2,1)S(1)}, bf16[3,38,512]{2,1,0:T(8,128)(2,1)S(1)}, u32[]{:S(2)}, u32[]{:S(2)}) collective-permute-start(bf16[3,38,512]{2,1,0:T(8,128)(2,1)S(1)} %get-tuple-element.236), channel_id=1, source_target_pairs={{0,128},{128,256},{256,384},{1,129},{129,257},{257,385},{2,130},{1... | collective-permute-start | bytes 350216 | tf_op jit(solution)/shard_map/ppermute | solution.py:26
  179.5 1.9 collective-permute-start.5
  181.5 1.0 convolution_convert_fusion.1
  182.4 3.5 slice.355
  186.0 3.7 collective-permute-done.5
  189.7 0.8 pad_maximum_fusion.5
  190.5 4.3 collective-permute-start.6
  194.9 1.5 collective-permute-start.7
  197.6 4.5 collective-permute-done.7
  202.0 1.7 fusion.42
  203.7 1.7 fusion.41
  205.4 1.2 convert_add_fusion.1
  206.6 3.8 scatter-add.39
  210.3 1.2 convert_add_fusion
  211.6 3.2 scatter-add.40
  214.7 0.8 convert_add_fusion.5
  215.6 1.5 scatter-add.41
  217.1 2.7 add_select_fusion
  219.8 2.8 scatter-add.44
  222.5 0.8 convert_add_fusion.4
  223.4 1.5 scatter-add.54
  224.9 0.8 slice_add_fusion
  225.7 1.5 scatter-add.55
  227.2 1.8 copy.86
  229.7 1.3 convolution_convert_fusion
  231.1 0.9 fusion.24
  232.0 2.1 fusion.25
  234.6 96.2 %all-reduce.1 = (f32[512]{0:T(512)}, f32[8,49]{1,0:T(8,128)}) all-reduce(f32[512]{0:T(512)S(1)} %get-tuple-element.204, f32[8,49]{1,0:T(8,128)S(1)} %fusion.25), channel_id=1, replica_groups=mesh['gy'=4,'gx'=4,'dp'=32] {'gy','gx','dp'}, use_global_device_ids=true, to_apply=%region_14.15 | all-reduce | flops 904 | bytes 7232 | tf_op jit(solution)/shard_map/psum | solution.py:248
  330.8 0.8 fusion.43
  331.6 66.2 %reduce-scatter.5.cloned.1.call-done = bf16[8,512]{1,0:T(8,128)(2,1)} async-done(((bf16[256,512]{1,0:T(8,128)(2,1)}), bf16[8,512]{1,0:T(8,128)(2,1)}) %reduce-scatter.5.cloned.1.call-update) | async-done | bytes 8208 | tf_op jit(solution)/shard_map/reduce_scatter | solution.py:257
  397.8 223.2 %reduce-scatter.3.cloned.1.call-done = bf16[16,768]{1,0:T(8,128)(2,1)} async-done(((bf16[512,768]{1,0:T(8,128)(2,1)}), bf16[16,768]{1,0:T(8,128)(2,1)}) %reduce-scatter.3.cloned.1.call-update) | async-done | bytes 24592 | tf_op jit(solution)/shard_map/reduce_scatter | solution.py:254
  621.0 59.8 %all-reduce.2 = (bf16[16,768]{1,0:T(8,128)(2,1)S(1)}, bf16[8,512]{1,0:T(8,128)(2,1)S(1)}) all-reduce(bf16[16,768]{1,0:T(8,128)(2,1)} %reduce-scatter.3.cloned.1.call-done, bf16[8,512]{1,0:T(8,128)(2,1)} %reduce-scatter.5.cloned.1.call-done), channel_id=1, replica_groups=mesh['gy'=4,'gx'=4,'dp'=32] {'gy','gx'}, use_global_device_ids=true, to_apply=%region_9.10 | all-reduce | flops 16384 | bytes 65536 | tf_op jit(solution)/shard_map/psum | solution.py:250
  (154 shorter events, 16.0 us)
Async XLA Ops:
  7.2 114.3 %copy-start = (f32[8,49]{1,0:T(8,128)S(1)}, f32[8,49]{1,0:T(8,128)}, u32[]{:S(2)}) copy-start(f32[8,49]{1,0:T(8,128)} %param.28) | copy-start | bytes 4708
  7.2 390.6 %reduce-scatter.5.cloned.1.call-start = ((), (), s32[]{:S(2)}) async-start(), calls=%async_computation.3 | async-start | bytes 270336 | tf_op jit(solution)/shard_map/reduce_scatter | solution.py:257
  49.8 1.4 copy-start.1
  51.9 25.6 %copy-start.21 = (s32[1,4,4,2]{2,3,1,0:T(2,128)S(1)}, s32[1,4,4,2]{2,3,1,0:T(2,128)}, u32[]{:S(2)}) copy-start(s32[1,4,4,2]{2,3,1,0:T(2,128)} %param.24) | copy-start | bytes 388
  51.9 33.0 %copy-start.20 = (bf16[8,512]{1,0:T(8,128)(2,1)S(1)}, bf16[8,512]{1,0:T(8,128)(2,1)}, u32[]{:S(2)}) copy-start(bf16[8,512]{1,0:T(8,128)(2,1)} %param.26) | copy-start | bytes 24580
  52.0 70.9 %copy-start.15 = (bf16[1,1,1,128,512]{4,3,2,1,0:T(8,128)(2,1)S(1)}, bf16[1,1,1,128,512]{4,3,2,1,0:T(8,128)(2,1)}, u32[]{:S(2)}) copy-start(bf16[1,1,1,128,512]{4,3,2,1,0:T(8,128)(2,1)} %param.29) | copy-start | bytes 393220
  52.2 71.0 %collective-permute-start = (bf16[3,32,512]{2,1,0:T(8,128)(2,1)S(1)}, bf16[3,32,512]{2,1,0:T(8,128)(2,1)S(1)}, u32[]{:S(2)}, u32[]{:S(2)}) collective-permute-start(bf16[3,32,512]{2,1,0:T(8,128)(2,1)S(1)} %get-tuple-element.240), channel_id=1, source_target_pairs={{0,128},{128,256},{256,384},{1,129},{129,257},{257,385},{2,130},{1... | collective-permute-start | bytes 294920 | tf_op jit(solution)/shard_map/ppermute | solution.py:26
  75.0 48.2 %collective-permute-start.1 = (bf16[3,32,512]{2,1,0:T(8,128)(2,1)S(1)}, bf16[3,32,512]{2,1,0:T(8,128)(2,1)S(1)}, u32[]{:S(2)}, u32[]{:S(2)}) collective-permute-start(bf16[3,32,512]{2,1,0:T(8,128)(2,1)S(1)} %get-tuple-element.241), channel_id=1, source_target_pairs={{128,0},{256,128},{384,256},{129,1},{257,129},{385,257},{130,2},{2... | collective-permute-start | bytes 294920 | tf_op jit(solution)/shard_map/ppermute | solution.py:27
  77.8 45.5 %copy-start.17 = (s32[64,196]{1,0:T(8,128)}, s32[64,196]{1,0:T(8,128)S(1)}, u32[]{:S(2)}) copy-start(s32[64,196]{1,0:T(8,128)S(1)} %fusion.57) | copy-start | bytes 150532
  78.6 44.6 %copy-start.22 = (pred[128]{0:T(512)(128)(4,1)}, pred[128]{0:T(512)(128)(4,1)S(1)}, u32[]{:S(2)}) copy-start(pred[128]{0:T(512)(128)(4,1)S(1)} %broadcast_in_dim.152) | copy-start | bytes 388
  120.7 2.2 copy-start.8
  122.9 6.1 copy-start.25
  123.3 6.4 collective-permute-start.2
  126.1 6.1 collective-permute-start.3
  129.0 15.1 %copy-start.6 = (bf16[2,64,8,32]{1,0,3,2:T(2,128)(2,1)}, bf16[2,64,8,32]{1,0,3,2:T(2,128)(2,1)S(1)}, u32[]{:S(2)}) copy-start(bf16[2,64,8,32]{1,0,3,2:T(2,128)(2,1)S(1)} %squeeze.40) | copy-start | bytes 196612
  129.7 0.7 copy-start.12
  139.5 2.2 copy-start.13
  139.5 2.8 copy-start.14
  141.5 2.6 copy-start.3
  143.1 0.9 copy-start.26
  146.3 1.2 copy-start.7
  156.0 25.4 %copy-start.10 = (bf16[128,256]{0,1:T(8,128)(2,1)S(1)}, bf16[128,256]{0,1:T(8,128)(2,1)}, u32[]{:S(2)}) copy-start(bf16[128,256]{0,1:T(8,128)(2,1)} %reshape.1052) | copy-start | bytes 196612
  156.0 25.4 %copy-start.16 = (bf16[1,1,1,128,512]{4,3,2,1,0:T(8,128)(2,1)S(1)}, bf16[1,1,1,128,512]{4,3,2,1,0:T(8,128)(2,1)}, u32[]{:S(2)}) copy-start(bf16[1,1,1,128,512]{4,3,2,1,0:T(8,128)(2,1)} %param.29) | copy-start | bytes 393220
  156.0 25.5 %copy-start.23 = (pred[128]{0:T(512)(128)(4,1)S(1)}, pred[128]{0:T(512)(128)(4,1)}, u32[]{:S(2)}) copy-start(pred[128]{0:T(512)(128)(4,1)} %copy-done.22) | copy-start | bytes 388
  158.1 27.8 %collective-permute-start.4 = (bf16[3,38,512]{2,1,0:T(8,128)(2,1)S(1)}, bf16[3,38,512]{2,1,0:T(8,128)(2,1)S(1)}, u32[]{:S(2)}, u32[]{:S(2)}) collective-permute-start(bf16[3,38,512]{2,1,0:T(8,128)(2,1)S(1)} %get-tuple-element.236), channel_id=1, source_target_pairs={{0,128},{128,256},{256,384},{1,129},{129,257},{257,385},{2,130},{1... | collective-permute-start | bytes 350216 | tf_op jit(solution)/shard_map/ppermute | solution.py:26
  179.5 10.2 %collective-permute-start.5 = (bf16[3,38,512]{2,1,0:T(8,128)(2,1)S(1)}, bf16[3,38,512]{2,1,0:T(8,128)(2,1)S(1)}, u32[]{:S(2)}, u32[]{:S(2)}) collective-permute-start(bf16[3,38,512]{2,1,0:T(8,128)(2,1)S(1)} %get-tuple-element.237), channel_id=1, source_target_pairs={{128,0},{256,128},{384,256},{129,1},{257,129},{385,257},{130,2},{2... | collective-permute-start | bytes 350216 | tf_op jit(solution)/shard_map/ppermute | solution.py:27
  185.9 10.5 %copy-start.4 = (bf16[2,196,256]{1,2,0:T(8,128)(2,1)S(1)}, bf16[2,196,256]{1,2,0:T(8,128)(2,1)}, u32[]{:S(2)}) copy-start(bf16[2,196,256]{1,2,0:T(8,128)(2,1)} %copy-done.3) | copy-start | bytes 602116
  185.9 435.0 %reduce-scatter.3.cloned.1.call-start = ((), (), s32[]{:S(2)}) async-start(), calls=%async_computation.2 | async-start | bytes 811008 | tf_op jit(solution)/shard_map/reduce_scatter | solution.py:254
  190.5 7.0 %collective-permute-start.6 = (bf16[44,3,512]{2,1,0:T(4,128)(2,1)}, bf16[44,3,512]{2,1,0:T(4,128)(2,1)S(1)}, u32[]{:S(2)}, u32[]{:S(2)}) collective-permute-start(bf16[44,3,512]{2,1,0:T(4,128)(2,1)} %get-tuple-element.234), channel_id=1, source_target_pairs={{0,32},{32,64},{64,96},{1,33},{33,65},{65,97},{2,34},{34,66},{66,9... | collective-permute-start | bytes 405512 | tf_op jit(solution)/shard_map/ppermute | solution.py:26
  194.9 7.2 %collective-permute-start.7 = (bf16[44,3,512]{2,1,0:T(4,128)(2,1)S(1)}, bf16[44,3,512]{2,1,0:T(4,128)(2,1)S(1)}, u32[]{:S(2)}, u32[]{:S(2)}) collective-permute-start(bf16[44,3,512]{2,1,0:T(4,128)(2,1)S(1)} %get-tuple-element.235), channel_id=1, source_target_pairs={{32,0},{64,32},{96,64},{33,1},{65,33},{97,65},{34,2},{66,34},{98,6... | collective-permute-start | bytes 405512 | tf_op jit(solution)/shard_map/ppermute | solution.py:27
  225.7 4.0 copy-start.5
  225.7 4.0 copy-start.19
  227.2 3.9 copy-start.9
  229.0 3.0 copy-start.11
  229.0 3.0 copy-start.18
  229.7 4.4 copy-start.2
  231.1 99.7 %copy-start.24 = (f32[128]{0:T(128)S(1)}, f32[128]{0:T(128)}, u32[]{:S(2)}) copy-start(f32[128]{0:T(128)} %get-tuple-element.244) | copy-start | bytes 1540
Sparse Core Ops, SparseCore 0:
  186.1 211.6 reduce-scatter.4
  402.8 218.1 reduce-scatter.2
where the time goes:
time: 690 us; the launch traced here: 689 us
  waiting for transfers between devices  300 us (43%)
  blocking collectives  232 us (34%)
  starting transfers between devices  58.1 us (8%)
  local copies, waits for them, and re-layouts  44.6 us (6%)
  other arithmetic  27.4 us (4%)
  between operations  14.9 us (2%)
  matrix products  12.1 us (2%)
    reduce_scatter x1, waiting for transfers between devices, shards(): lax.psum_scatter(qkv_whole.astype(jnp.bfloat16), 'dp', scatter_dimension=...  223 us
    psum x1, blocking collectives, shards(): lax.psum((gain_local, bias_local), ('gy', 'gx', 'dp'))  96.2 us
    reduce_scatter x1, waiting for transfers between devices, shards(): lax.psum_scatter(out_whole.astype(jnp.bfloat16), 'dp', scatter_dimension=...  66.2 us
    psum x1, blocking collectives, shards(): lax.psum(grad_qkv_local.astype(jnp.bfloat16), ('gy', 'gx'))  59.8 us
    ppermute x4, starting transfers between devices, padded_2(): before = lax.ppermute(last, axis, up)  51.2 us
    all_gather x1, blocking collectives, shards(): lax.all_gather(w_qkv, 'dp', axis=0, tiled=True)  40.1 us
    all_gather x1, blocking collectives, shards(): lax.all_gather(w_out, 'dp', axis=0, tiled=True)  35.8 us
  transfers between devices with their start and end apart: 10, of which 6 were waited for; matrix products, arithmetic and copies ran while one was open for 7% of the time, Pallas kernels for 0%

commit v1 on v0

--- a/solution.py
+++ b/solution.py
@@ -70,7 +70,9 @@
     bias_table = jnp.einsum("ho,oqk->hqk", rel_bias, onehot, precision=lax.Precision.HIGHEST)
     w_qkv_all, w_out_all = (
         lax.all_gather(w_qkv, "dp", axis=0, tiled=True),
-        lax.all_gather(w_out, "dp", axis=0, tiled=True),
+        jnp.concatenate(
+            lax.all_to_all(jnp.stack([w_out] * lax.axis_size("dp")), "dp", 0, 0), axis=0
+        ),
     )
     features = tokens.reshape(ROWS, D).astype(jnp.float32)
     inv_rms = lax.rsqrt(jnp.mean(features * features, axis=-1, keepdims=True) + 1e-06)

time: 690 us -> 652 us (0.945)
  blocking collectives: 232 us -> 195 us
    all_gather x1 -> x0, blocking collectives: 35.8 us -> none  [shards(): lax.all_gather(w_out, 'dp', axis=0, tiled=True)]
    ppermute x4, starting transfers between devices: 51.2 us -> 39.2 us  [padded_2(): before = lax.ppermute(last, axis, up)]
    all_to_all x0 -> x1, starting transfers between devices: none -> 10.5 us  [shards(): lax.all_to_all(jnp.stack([w_out] * lax.axis_size('dp')), 'dp', 0, 0)]
  transfers between devices with their start and end apart: 10 -> 11, of which waited for: 6 -> 6; matrix products, arithmetic and copies ran while one was open for 7% -> 11% of each run, Pallas kernels for 0% -> 0%
where the time goes in v1:
time: 652 us; the launch traced here: 650 us
  waiting for transfers between devices  296 us (45%)
  blocking collectives  195 us (30%)
  starting transfers between devices  56.6 us (9%)
  local copies, waits for them, and re-layouts  47.6 us (7%)
  other arithmetic  27.5 us (4%)
  between operations  14.9 us (2%)
  matrix products  12.1 us (2%)
    reduce_scatter x1, waiting for transfers between devices, shards(): lax.psum_scatter(qkv_whole.astype(jnp.bfloat16), 'dp', scatter_dimension=...  223 us
    psum x1, blocking collectives, shards(): lax.psum((gain_local, bias_local), ('gy', 'gx', 'dp'))  96.5 us
    reduce_scatter x1, waiting for transfers between devices, shards(): lax.psum_scatter(out_whole.astype(jnp.bfloat16), 'dp', scatter_dimension=...  63.4 us
    psum x1, blocking collectives, shards(): lax.psum(grad_qkv_local.astype(jnp.bfloat16), ('gy', 'gx'))  59.8 us
    ppermute x4, starting transfers between devices, padded_2(): before = lax.ppermute(last, axis, up)  39.2 us
    all_gather x1, blocking collectives, shards(): lax.all_gather(w_qkv, 'dp', axis=0, tiled=True)  39.1 us
  transfers between devices with their start and end apart: 11, of which 6 were waited for; matrix products, arithmetic and copies ran while one was open for 11% of the time, Pallas kernels for 0%

profile of v1, /device:TPU:1, one launch (start us, length us, event | category | flops | bytes accessed | tf_op | source)
XLA Modules:
  0.0 650.0 jit_solution(3756850234880267005)
XLA Ops:
  7.2 1.4 stack.2
  8.6 10.5 %all-to-all-start = ((bf16[32,8,512]{2,1,0:T(8,128)(2,1)}), bf16[32,8,512]{2,1,0:T(8,128)(2,1)S(1)}, u32[]{:S(2)}, u32[]{:S(2)}) async-start(bf16[32,8,512]{2,1,0:T(8,128)(2,1)} %stack.2), calls=%async_computation | async-start | bytes 524288 | tf_op jit(solution)/shard_map/all_to_all | solution.py:74
  19.2 1.0 fusion.29
  20.7 0.9 dynamic-slice_reduce_fusion
  21.6 39.1 %all_gather.3 = bf16[512,768]{1,0:T(8,128)(2,1)S(1)} all-gather(bf16[16,768]{1,0:T(8,128)(2,1)} %param.25), channel_id=1, replica_groups=mesh['gy'=4,'gx'=4,'dp'=32] {'dp'}, dimensions={0}, use_global_device_ids=true | all-gather | bytes 811008 | tf_op jit(solution)/shard_map/all_gather | solution.py:72
  60.6 1.3 convolution_convert_fusion.2
  63.0 22.8 %collective-permute-start = (bf16[3,32,512]{2,1,0:T(8,128)(2,1)S(1)}, bf16[3,32,512]{2,1,0:T(8,128)(2,1)S(1)}, u32[]{:S(2)}, u32[]{:S(2)}) collective-permute-start(bf16[3,32,512]{2,1,0:T(8,128)(2,1)S(1)} %get-tuple-element.240), channel_id=1, source_target_pairs={{0,128},{128,256},{256,384},{1,129},{129,257},{257,385},{2,130},{1... | collective-permute-start | bytes 294920 | tf_op jit(solution)/shard_map/ppermute | solution.py:26
  85.8 1.9 collective-permute-start.1
  90.1 0.7 scatter_custom_fusion.1
  91.3 4.2 while.21
  91.9 1.4 dynamic-slice.90
  94.0 1.4 dynamic-slice.90
  96.3 1.4 fusion.16
  98.0 3.1 collective-permute-start.2
  101.1 1.5 collective-permute-start.3
  104.4 0.7 and_reduce_fusion
  105.8 1.3 collective-permute-done.3
  107.1 2.0 pad_maximum_fusion
  109.1 6.8 %while.20 = (s32[]{:T(128)}, bf16[38,38,512]{2,1,0:T(8,128)(2,1)S(1)}, s32[2,3]{1,0:T(2,128)}, bf16[2,14,14,512]{3,2,1,0:T(8,128)(2,1)}, s32[]{:T(128)}) while((s32[]{:T(128)}, bf16[38,38,512]{2,1,0:T(8,128)(2,1)S(1)}, s32[2,3]{1,0:T(2,128)}, bf16[2,14,14,512]{3,2,1,0:T(8,128)(2,1)}, s32[]{:T(128)}) %tuple.102), condition=%wide.while_cond.8, body=%wide.while_body.8.sunk | while | flops 2 | bytes 431221 | solution.py:124
  109.1 0.7 constant_dynamic-slice_fusion.4
  110.4 2.1 bitcast_dynamic-update-slice_fusion.4
  112.5 0.7 constant_dynamic-slice_fusion.4
  113.8 2.1 bitcast_dynamic-update-slice_fusion.4
  115.9 1.4 copy.67
  118.7 0.8 fusion.23
  119.7 0.7 reshape.1063
  121.0 0.8 convolution_bitcast_fusion
  123.2 1.2 convert_reduce_fusion
  125.5 1.2 copy.85
  126.7 4.2 scatter_custom_fusion.2
  130.9 2.0 reshape.1067
  132.9 2.1 convert_element_type.82
  135.0 9.0 %collective-permute-start.4 = (bf16[3,38,512]{2,1,0:T(8,128)(2,1)S(1)}, bf16[3,38,512]{2,1,0:T(8,128)(2,1)S(1)}, u32[]{:S(2)}, u32[]{:S(2)}) collective-permute-start(bf16[3,38,512]{2,1,0:T(8,128)(2,1)S(1)} %get-tuple-element.236), channel_id=1, source_target_pairs={{0,128},{128,256},{256,384},{1,129},{129,257},{257,385},{2,130},{1... | collective-permute-start | bytes 350216 | tf_op jit(solution)/shard_map/ppermute | solution.py:26
  144.0 1.9 collective-permute-start.5
  146.0 1.0 convolution_convert_fusion.1
  147.0 3.5 slice.355
  150.5 3.7 collective-permute-done.5
  154.2 0.8 pad_maximum_fusion.5
  155.0 4.3 collective-permute-start.6
  159.4 1.5 collective-permute-start.7
  162.1 3.7 collective-permute-done.7
  165.8 1.7 fusion.44
  167.5 1.6 fusion.43
  169.1 1.2 convert_add_fusion.1
  170.3 3.8 scatter-add.39
  174.1 1.2 convert_add_fusion
  175.4 3.2 scatter-add.40
  178.5 0.8 convert_add_fusion.5
  179.4 1.5 scatter-add.41
  180.8 2.7 add_select_fusion
  183.5 2.6 scatter-add.44
  186.1 0.8 convert_add_fusion.4
  186.9 1.5 scatter-add.54
  188.4 0.8 slice_add_fusion
  189.3 1.5 scatter-add.55
  190.8 1.8 copy.86
  193.3 1.4 convolution_convert_fusion
  194.7 0.9 fusion.24
  195.6 2.1 fusion.25
  198.2 96.5 %all-reduce.1 = (f32[512]{0:T(512)}, f32[8,49]{1,0:T(8,128)}) all-reduce(f32[512]{0:T(512)S(1)} %get-tuple-element.204, f32[8,49]{1,0:T(8,128)S(1)} %fusion.25), channel_id=1, replica_groups=mesh['gy'=4,'gx'=4,'dp'=32] {'gy','gx','dp'}, use_global_device_ids=true, to_apply=%region_14.15 | all-reduce | flops 904 | bytes 7232 | tf_op jit(solution)/shard_map/psum | solution.py:250
  294.7 0.8 fusion.45
  295.5 63.4 %reduce-scatter.5.cloned.1.call-done = bf16[8,512]{1,0:T(8,128)(2,1)} async-done(((bf16[256,512]{1,0:T(8,128)(2,1)}), bf16[8,512]{1,0:T(8,128)(2,1)}) %reduce-scatter.5.cloned.1.call-update) | async-done | bytes 8208 | tf_op jit(solution)/shard_map/reduce_scatter | solution.py:259
  358.9 223.3 %reduce-scatter.3.cloned.1.call-done = bf16[16,768]{1,0:T(8,128)(2,1)} async-done(((bf16[512,768]{1,0:T(8,128)(2,1)}), bf16[16,768]{1,0:T(8,128)(2,1)}) %reduce-scatter.3.cloned.1.call-update) | async-done | bytes 24592 | tf_op jit(solution)/shard_map/reduce_scatter | solution.py:256
  582.2 59.8 %all-reduce.2 = (bf16[16,768]{1,0:T(8,128)(2,1)S(1)}, bf16[8,512]{1,0:T(8,128)(2,1)S(1)}) all-reduce(bf16[16,768]{1,0:T(8,128)(2,1)} %reduce-scatter.3.cloned.1.call-done, bf16[8,512]{1,0:T(8,128)(2,1)} %reduce-scatter.5.cloned.1.call-done), channel_id=1, replica_groups=mesh['gy'=4,'gx'=4,'dp'=32] {'gy','gx'}, use_global_device_ids=true, to_apply=%region_9.10 | all-reduce | flops 16384 | bytes 65536 | tf_op jit(solution)/shard_map/psum | solution.py:252
  (156 shorter events, 18.5 us)
Async XLA Ops:
  7.2 89.2 %copy-start = (f32[8,49]{1,0:T(8,128)S(1)}, f32[8,49]{1,0:T(8,128)}, u32[]{:S(2)}) copy-start(f32[8,49]{1,0:T(8,128)} %param.28) | copy-start | bytes 4708
  8.6 111.9 %all-to-all-start = ((bf16[32,8,512]{2,1,0:T(8,128)(2,1)}), bf16[32,8,512]{2,1,0:T(8,128)(2,1)S(1)}, u32[]{:S(2)}, u32[]{:S(2)}) async-start(bf16[32,8,512]{2,1,0:T(8,128)(2,1)} %stack.2), calls=%async_computation | async-start | bytes 524288 | tf_op jit(solution)/shard_map/all_to_all | solution.py:74
  19.1 339.8 %reduce-scatter.5.cloned.1.call-start = ((), (), s32[]{:S(2)}) async-start(), calls=%async_computation.4 | async-start | bytes 270336 | tf_op jit(solution)/shard_map/reduce_scatter | solution.py:259
  60.6 1.4 copy-start.1
  62.7 25.7 %copy-start.21 = (s32[1,4,4,2]{2,3,1,0:T(2,128)S(1)}, s32[1,4,4,2]{2,3,1,0:T(2,128)}, u32[]{:S(2)}) copy-start(s32[1,4,4,2]{2,3,1,0:T(2,128)} %param.24) | copy-start | bytes 388
  63.0 34.8 %collective-permute-start = (bf16[3,32,512]{2,1,0:T(8,128)(2,1)S(1)}, bf16[3,32,512]{2,1,0:T(8,128)(2,1)S(1)}, u32[]{:S(2)}, u32[]{:S(2)}) collective-permute-start(bf16[3,32,512]{2,1,0:T(8,128)(2,1)S(1)} %get-tuple-element.240), channel_id=1, source_target_pairs={{0,128},{128,256},{256,384},{1,129},{129,257},{257,385},{2,130},{1... | collective-permute-start | bytes 294920 | tf_op jit(solution)/shard_map/ppermute | solution.py:26
  85.8 12.0 %collective-permute-start.1 = (bf16[3,32,512]{2,1,0:T(8,128)(2,1)S(1)}, bf16[3,32,512]{2,1,0:T(8,128)(2,1)S(1)}, u32[]{:S(2)}, u32[]{:S(2)}) collective-permute-start(bf16[3,32,512]{2,1,0:T(8,128)(2,1)S(1)} %get-tuple-element.241), channel_id=1, source_target_pairs={{128,0},{256,128},{384,256},{129,1},{257,129},{385,257},{130,2},{2... | collective-permute-start | bytes 294920 | tf_op jit(solution)/shard_map/ppermute | solution.py:27
  88.8 9.0 %copy-start.18 = (s32[64,196]{1,0:T(8,128)}, s32[64,196]{1,0:T(8,128)S(1)}, u32[]{:S(2)}) copy-start(s32[64,196]{1,0:T(8,128)S(1)} %fusion.57) | copy-start | bytes 150532
  96.3 8.1 %copy-start.25 = (s32[3]{0:T(128)S(1)}, s32[3]{0:T(128)}, u32[]{:S(2)}) copy-start(s32[3]{0:T(128)} %constant.428.clone.1) | copy-start | bytes 40
  97.8 7.4 %copy-start.12 = (bf16[3,32,512]{2,1,0:T(8,128)(2,1)}, bf16[3,32,512]{2,1,0:T(8,128)(2,1)S(1)}, u32[]{:S(2)}) copy-start(bf16[3,32,512]{2,1,0:T(8,128)(2,1)S(1)} %collective-permute-done) | copy-start | bytes 294916
  97.8 7.3 %copy-start.13 = (bf16[3,32,512]{2,1,0:T(8,128)(2,1)}, bf16[3,32,512]{2,1,0:T(8,128)(2,1)S(1)}, u32[]{:S(2)}) copy-start(bf16[3,32,512]{2,1,0:T(8,128)(2,1)S(1)} %collective-permute-done.1) | copy-start | bytes 294916
  98.0 7.2 %collective-permute-start.2 = (bf16[38,3,512]{2,1,0:T(4,128)(2,1)S(1)}, bf16[38,3,512]{2,1,0:T(4,128)(2,1)S(1)}, u32[]{:S(2)}, u32[]{:S(2)}) collective-permute-start(bf16[38,3,512]{2,1,0:T(4,128)(2,1)S(1)} %get-tuple-element.238), channel_id=1, source_target_pairs={{0,32},{32,64},{64,96},{1,33},{33,65},{65,97},{2,34},{34,66},{66,9... | collective-permute-start | bytes 350216 | tf_op jit(solution)/shard_map/ppermute | solution.py:26
  101.1 6.1 collective-permute-start.3
  104.4 16.5 %copy-start.6 = (bf16[2,64,8,32]{1,0,3,2:T(2,128)(2,1)}, bf16[2,64,8,32]{1,0,3,2:T(2,128)(2,1)S(1)}, u32[]{:S(2)}) copy-start(bf16[2,64,8,32]{1,0,3,2:T(2,128)(2,1)S(1)} %squeeze.40) | copy-start | bytes 196612
  105.2 0.7 copy-start.14
  115.9 2.1 copy-start.15
  115.9 2.8 copy-start.26
  117.8 3.1 copy-start.3
  118.7 1.8 copy-start.16
  118.7 1.8 copy-start.22
  120.5 1.3 copy-start.8
  123.2 1.2 copy-start.7
  132.9 13.1 %copy-start.10 = (bf16[128,256]{0,1:T(8,128)(2,1)S(1)}, bf16[128,256]{0,1:T(8,128)(2,1)}, u32[]{:S(2)}) copy-start(bf16[128,256]{0,1:T(8,128)(2,1)} %reshape.1063) | copy-start | bytes 196612
  132.9 13.1 %copy-start.17 = (bf16[1,1,1,128,512]{4,3,2,1,0:T(8,128)(2,1)S(1)}, bf16[1,1,1,128,512]{4,3,2,1,0:T(8,128)(2,1)}, u32[]{:S(2)}) copy-start(bf16[1,1,1,128,512]{4,3,2,1,0:T(8,128)(2,1)} %param.29) | copy-start | bytes 393220
  132.9 13.1 %copy-start.23 = (pred[128]{0:T(512)(128)(4,1)S(1)}, pred[128]{0:T(512)(128)(4,1)}, u32[]{:S(2)}) copy-start(pred[128]{0:T(512)(128)(4,1)} %broadcast_in_dim.150) | copy-start | bytes 388
  135.0 15.5 %collective-permute-start.4 = (bf16[3,38,512]{2,1,0:T(8,128)(2,1)S(1)}, bf16[3,38,512]{2,1,0:T(8,128)(2,1)S(1)}, u32[]{:S(2)}, u32[]{:S(2)}) collective-permute-start(bf16[3,38,512]{2,1,0:T(8,128)(2,1)S(1)} %get-tuple-element.236), channel_id=1, source_target_pairs={{0,128},{128,256},{256,384},{1,129},{129,257},{257,385},{2,130},{1... | collective-permute-start | bytes 350216 | tf_op jit(solution)/shard_map/ppermute | solution.py:26
  144.0 10.2 %collective-permute-start.5 = (bf16[3,38,512]{2,1,0:T(8,128)(2,1)S(1)}, bf16[3,38,512]{2,1,0:T(8,128)(2,1)S(1)}, u32[]{:S(2)}, u32[]{:S(2)}) collective-permute-start(bf16[3,38,512]{2,1,0:T(8,128)(2,1)S(1)} %get-tuple-element.237), channel_id=1, source_target_pairs={{128,0},{256,128},{384,256},{129,1},{257,129},{385,257},{130,2},{2... | collective-permute-start | bytes 350216 | tf_op jit(solution)/shard_map/ppermute | solution.py:27
  147.0 435.2 %reduce-scatter.3.cloned.1.call-start = ((), (), s32[]{:S(2)}) async-start(), calls=%async_computation.3 | async-start | bytes 811008 | tf_op jit(solution)/shard_map/reduce_scatter | solution.py:256
  150.5 10.3 %copy-start.4 = (bf16[2,196,256]{1,2,0:T(8,128)(2,1)S(1)}, bf16[2,196,256]{1,2,0:T(8,128)(2,1)}, u32[]{:S(2)}) copy-start(bf16[2,196,256]{1,2,0:T(8,128)(2,1)} %copy-done.3) | copy-start | bytes 602116
  155.0 7.0 %collective-permute-start.6 = (bf16[44,3,512]{2,1,0:T(4,128)(2,1)}, bf16[44,3,512]{2,1,0:T(4,128)(2,1)S(1)}, u32[]{:S(2)}, u32[]{:S(2)}) collective-permute-start(bf16[44,3,512]{2,1,0:T(4,128)(2,1)} %get-tuple-element.234), channel_id=1, source_target_pairs={{0,32},{32,64},{64,96},{1,33},{33,65},{65,97},{2,34},{34,66},{66,9... | collective-permute-start | bytes 405512 | tf_op jit(solution)/shard_map/ppermute | solution.py:26
  159.4 6.4 collective-permute-start.7
  189.3 4.0 copy-start.5
  189.3 4.0 copy-start.20
  190.8 3.9 copy-start.9
  192.6 3.0 copy-start.11
  192.6 3.0 copy-start.19
  193.3 4.4 copy-start.2
  194.7 100.0 %copy-start.24 = (f32[128]{0:T(128)S(1)}, f32[128]{0:T(128)}, u32[]{:S(2)}) copy-start(f32[128]{0:T(128)} %get-tuple-element.244) | copy-start | bytes 1540
Sparse Core Ops, SparseCore 0:
  147.1 211.7 reduce-scatter.4
  363.9 218.2 reduce-scatter.2
